TPU v7x, 32 devices: a whole 2x2x4 slice. The times are simulated.
32 devices in a mesh: tm: 2 (over y), mesh: 16 (over z, x, core).
Axes of the slice: x: 2, y: 2, z: 4, core: 2. Of those that a mesh axis runs over, the one named last changes fastest.
Arguments:
- inverse: bfloat16 [2, 135, 135, 2048], P('tm', None, None, 'mesh'), may hold values from -0.3 to 1.9
- start: float32 [2, 135, 2048], P('tm', None, 'mesh'), may hold values from -6 to 6
- source: float32 [2, 135, 2048], P('tm', None, 'mesh'), may hold values from -6 to 6
- mass: float32 [135, 2048], P(None, 'mesh'), may hold values from 0.1 to 1
- inner_elem: int32 [2, 4096], P(None, 'mesh'), may hold values from 0 to 127
- inner_face: int32 [2, 4096], P(None, 'mesh'), may hold values from 0 to 5
- inner_orient: int32 [4096], P('mesh'), may hold values from 0 to 7
- inner_jac: float32 [2, 2, 25, 4096], P('tm', None, None, 'mesh'), may hold values from -0.72 to 0.72
- cross_elem: int32 [16, 160], P('mesh'), may hold values from 0 to 127
- cross_face: int32 [16, 160], P('mesh'), may hold values from 0 to 5
- cross_orient: int32 [16, 160], P('mesh'), may hold values from 0 to 7, as said below
- cross_count: int32 [16, 5], P('mesh'), may hold values from 1 to 32, as said below
- cross_jac: float32 [2, 25, 16, 160], P('tm', None, 'mesh'), may hold values from -0.72 to 0.72
Outputs:
- adjoint: float32 [2, 135, 2048], P('tm', None, 'mesh')
Inputs may be any that keep to these rules, and one draw needn't show every extreme that they name: cross_count[(p + off[k]) mod 16, mirror[k]] = cross_count[p, k], and cross_count[p, 3] = 32. cross_orient[(p + off[k]) mod 16, mirror[k] * 32 + s] = inv(cross_orient[p, k * 32 + s]).
All inputs are finite; a program needn't handle non-finite values.
Results may differ from a plain program's by a relative error of at most 0.008.
Values sent between devices are 32-bit elements; how exact they have to be, the bound alone decides.
A program may use at most 128 MiB of HBM per device.

v0:
```python
import functools
import math

import jax
import jax.numpy as jnp
import numpy as np
from jax import lax
from jax.experimental import pallas as pl
from jax.experimental.pallas import tpu as pltpu
from jax.sharding import PartitionSpec as P

SWEEPS = 2
VARS = 5
NODES = 27
MIRROR = (1, 0, 4, 3, 2)
LINE_WEIGHTS = (1.0 / 3.0, 4.0 / 3.0, 1.0 / 3.0)
MESH = pl.DeviceIdType.MESH


def face_table():
    nodes = [[0] * 9 for _ in range(6)]
    weight = [1.0] * NODES
    for face in range(6):
        normal = face // 2
        tangent = [axis for axis in range(3) if axis != normal]
        for j in range(3):
            for i in range(3):
                coords = [0, 0, 0]
                coords[normal] = 2 * (face % 2)
                coords[tangent[0]] = i
                coords[tangent[1]] = j
                node = 9 * coords[2] + 3 * coords[1] + coords[0]
                nodes[face][3 * j + i] = node
                weight[node] = float(np.float32(LINE_WEIGHTS[i] * LINE_WEIGHTS[j]))
    return nodes, weight


FACE_NODES, NODE_WEIGHT = face_table()


def coef_table(count):
    table = [0.0] * count
    for k in range(1, count):
        parity = (-1.0) ** k
        phase = math.pi * k / count
        table[k] = 0.3 * parity * math.cos(phase) / math.sin(phase) + 1.2 * parity / count
    return [float(np.float32(c)) for c in table]


def split_rows(value):
    high = value.astype(jnp.bfloat16).astype(jnp.float32)
    return jnp.concatenate([high, value - high], axis=0).astype(jnp.bfloat16)


def orient_back(orient):
    swapped = 4 + 2 * (orient & 1) + ((orient >> 1) & 1)
    return jnp.where(orient >= 4, swapped, orient)


def apply_orient(trace, orient):
    shape = trace[0].shape
    flip_i = jnp.broadcast_to((orient & 1) == 1, shape)
    flip_j = jnp.broadcast_to((orient & 2) == 2, shape)
    swap = jnp.broadcast_to(orient >= 4, shape)
    step = [
        trace[3 * j + i] if i == 1 else jnp.where(flip_i, trace[3 * j + 2 - i], trace[3 * j + i])
        for j in range(3)
        for i in range(3)
    ]
    step = [
        step[3 * j + i] if j == 1 else jnp.where(flip_j, step[3 * (2 - j) + i], step[3 * j + i])
        for j in range(3)
        for i in range(3)
    ]
    return [
        step[3 * j + i] if i == j else jnp.where(swap, step[3 * i + j], step[3 * j + i])
        for j in range(3)
        for i in range(3)
    ]


def apply_jacobian(jac, trace):
    received = []
    for value in trace:
        total = jac[0] * value[0:1, :]
        for u in range(1, VARS):
            total = total + jac[u] * value[u : u + 1, :]
        received.append(total)
    return received


def kernel(
    count_times,
    count_mesh,
    inverse,
    start,
    source,
    mass,
    inner_elem,
    inner_face,
    inner_orient,
    inner_jac,
    cross_elem,
    cross_face,
    cross_orient,
    cross_count,
    cross_jac,
    out,
    inv_v,
    hot_inner,
    hot_cross,
    state,
    jac,
    couple,
    resid,
    current,
    send_buf,
    recv_buf,
    peer_buf,
    inv_sem,
    send_sem,
    recv_sem,
    peer_send_sem,
    peer_recv_sem,
):
    elems = start.shape[1]
    fin = inner_orient.shape[1]
    slots = cross_orient.shape[1]
    cap = slots // 5
    lanes = hot_cross.shape[1]
    chunk = inv_v.shape[0] // 5
    me = lax.axis_index("mesh")
    mine = lax.axis_index("tm")
    offsets = [1, count_mesh - 1, count_mesh // 2 - 1, count_mesh // 2, count_mesh // 2 + 1]
    partners = [lax.rem(me + off, count_mesh) for off in offsets]
    peers = [lax.rem(mine - d + count_times, count_times) for d in range(1, count_times)]
    coef = coef_table(count_times)

    loads = [
        pltpu.make_async_copy(
            inverse.at[pl.ds(c * chunk, chunk)], inv_v.at[pl.ds(c * chunk, chunk)], inv_sem.at[c]
        )
        for c in range(5)
    ]
    for load in loads:
        load.start()

    barrier = pltpu.get_barrier_semaphore()
    for partner in partners:
        pl.semaphore_signal(barrier, inc=1, device_id={"mesh": partner}, device_id_type=MESH)
    for peer in peers:
        pl.semaphore_signal(barrier, inc=1, device_id={"tm": peer}, device_id_type=MESH)

    cross_key = cross_face[...] * elems + cross_elem[...]
    cross_key = jnp.concatenate(
        [cross_key, jnp.full((1, lanes - slots), -1, jnp.int32)], axis=1
    )
    inner_key = inner_face[...] * elems + inner_elem[...]
    inner_key = jnp.concatenate([inner_key[0:1], inner_key[1:2]], axis=1)
    for face in range(6):
        rows = lax.broadcasted_iota(jnp.int32, (elems, lanes), 0) + face * elems
        hot_cross[pl.ds(face * elems, elems), :] = jnp.where(
            rows == cross_key, 1.0, 0.0
        ).astype(jnp.bfloat16)
        rows = lax.broadcasted_iota(jnp.int32, (elems, 2 * fin), 0) + face * elems
        hot_inner[pl.ds(face * elems, elems), :] = jnp.where(
            rows == inner_key, 1.0, 0.0
        ).astype(jnp.bfloat16)

    jac[...] = jnp.zeros_like(jac)
    for u in range(VARS):
        for v in range(VARS):
            jac[u, v : v + 1, 0:fin] = inner_jac[5 * u + v, 0:1, :]
            jac[u, v : v + 1, fin : 2 * fin] = inner_jac[5 * u + v, 1:2, :]
            jac[u, v : v + 1, 2 * fin : 2 * fin + slots] = cross_jac[5 * u + v, :, :]

    orient = inner_orient[...]
    inner_orients = jnp.concatenate([orient, orient_back(orient)], axis=1)
    cross_orients = jnp.concatenate(
        [cross_orient[...], jnp.zeros((1, lanes - slots), jnp.int32)], axis=1
    )
    lane = lax.broadcasted_iota(jnp.int32, (1, lanes), 1)
    live = jnp.zeros((1, lanes), jnp.int32)
    for k in range(5):
        live = jnp.where((lane >= k * cap) & (lane < k * cap + cross_count[0, k]), 1, live)
    live = jnp.broadcast_to(live == 1, (8, lanes))
    group = lax.broadcasted_iota(jnp.int32, (8, 128), 1) // cap

    state[...] = jnp.zeros_like(state)
    resid[...] = jnp.zeros_like(resid)
    zero_tile = jnp.zeros((8, 128), jnp.float32)

    for sweep in range(SWEEPS):
        now = start if sweep == 0 else current
        for v in range(VARS):
            state[pl.ds(v, NODES, stride=8), :] = now[v * NODES : (v + 1) * NODES, :]
        peer_copies = [
            pltpu.make_async_remote_copy(
                src_ref=now,
                dst_ref=peer_buf.at[sweep, d],
                send_sem=peer_send_sem.at[sweep, d],
                recv_sem=peer_recv_sem.at[sweep, d],
                device_id={"tm": peers[d]},
                device_id_type=MESH,
            )
            for d in range(count_times - 1)
        ]
        if sweep > 0:
            for copy in peer_copies:
                copy.start()
        tiles = [
            state[8 * node : 8 * node + 8, :] * NODE_WEIGHT[node] for node in range(NODES)
        ]
        faces = jnp.concatenate(
            [
                jnp.concatenate([tiles[FACE_NODES[face][n]] for face in range(6)], axis=1)
                for n in range(9)
            ],
            axis=0,
        )
        faces = split_rows(faces)

        cross_trace = jnp.dot(faces, hot_cross[...], preferred_element_type=jnp.float32)
        cross_trace = cross_trace[0:72] + cross_trace[72:144]
        for k in range(5):
            column = (k // 4) * 128
            for h in range(3):
                packed = zero_tile
                for g in range(4):
                    n = 4 * h + g
                    if n < 9:
                        piece = cross_trace[8 * n : 8 * n + 8, column : column + 128]
                        shift = (g - k % 4) * cap % 128
                        piece = pltpu.roll(piece, shift, 1) if shift else piece
                        packed = jnp.where(group == g, piece, packed)
                send_buf[sweep, k, 8 * h : 8 * h + 8, :] = packed
        if sweep == 0:
            pl.semaphore_wait(barrier, 5 + count_times - 1)
        copies = [
            pltpu.make_async_remote_copy(
                src_ref=send_buf.at[sweep, k],
                dst_ref=recv_buf.at[sweep, MIRROR[k]],
                send_sem=send_sem.at[sweep, k],
                recv_sem=recv_sem.at[sweep, MIRROR[k]],
                device_id={"mesh": partners[k]},
                device_id_type=MESH,
            )
            for k in range(5)
        ]
        for k in (3, 2, 4, 0, 1):
            copies[k].start()
        if sweep == 0:
            for copy in peer_copies:
                copy.start()

        trace = jnp.dot(faces, hot_inner[...], preferred_element_type=jnp.float32)
        trace = trace[0:72] + trace[72:144]
        trace = [
            jnp.concatenate(
                [trace[8 * n : 8 * n + 8, fin:], trace[8 * n : 8 * n + 8, :fin]], axis=1
            )
            for n in range(9)
        ]
        trace = apply_orient(trace, inner_orients)
        received = apply_jacobian([jac[u, :, 0 : 2 * fin] for u in range(VARS)], trace)
        received = split_rows(jnp.concatenate(received, axis=0))
        placed = lax.dot_general(
            received,
            hot_inner[...],
            (((1,), (1,)), ((), ())),
            preferred_element_type=jnp.float32,
        )
        inner_placed = placed[0:72] + placed[72:144]

        for copy in copies:
            copy.wait_recv()
        arrived = []
        for n in range(9):
            h, g = n // 4, n % 4
            columns = [zero_tile] * (lanes // 128)
            for k in range(5):
                piece = recv_buf[sweep, k, 8 * h : 8 * h + 8, :]
                shift = (k % 4 - g) * cap % 128
                piece = pltpu.roll(piece, shift, 1) if shift else piece
                columns[k // 4] = jnp.where(group == k % 4, piece, columns[k // 4])
            arrived.append(jnp.concatenate(columns, axis=1))
        arrived = apply_orient(arrived, cross_orients)
        received = apply_jacobian([jac[u, :, 2 * fin :] for u in range(VARS)], arrived)
        received = [jnp.where(live, value, 0.0) for value in received]
        received = split_rows(jnp.concatenate(received, axis=0))
        placed = lax.dot_general(
            received,
            hot_cross[...],
            (((1,), (1,)), ((), ())),
            preferred_element_type=jnp.float32,
        )
        placed = placed[0:72] + placed[72:144] + inner_placed

        totals = [zero_tile] * NODES
        for face in range(6):
            for n in range(9):
                node = FACE_NODES[face][n]
                totals[node] = (
                    totals[node] + placed[8 * n : 8 * n + 8, face * elems : (face + 1) * elems]
                )
        for node in range(NODES):
            couple[8 * node : 8 * node + 8, :] = totals[node]

        for copy in peer_copies:
            copy.wait_recv()
        for v in range(VARS):
            rows = slice(v * NODES, (v + 1) * NODES)
            spectral = coef[1] * peer_buf[sweep, 0, rows, :]
            for d in range(1, count_times - 1):
                spectral = spectral + coef[d + 1] * peer_buf[sweep, d, rows, :]
            value = (
                source[rows, :]
                - couple[pl.ds(v, NODES, stride=8), :]
                - mass[rows, :] * spectral
            )
            resid[rows, :] = value.astype(jnp.bfloat16).astype(jnp.float32)

        for copy in peer_copies:
            copy.wait_send()
        for copy in copies:
            copy.wait_send()
        if sweep == 0:
            for load in loads:
                load.wait()
        target = out if sweep == SWEEPS - 1 else current
        top = resid[0:128, :].reshape(16, 8, 128)
        tail = resid[128:136, :]

        def row_sum(row):
            block = inv_v[row, 0:128, :].astype(jnp.float32).reshape(16, 8, 128)
            last = inv_v[row, 128:135, :].astype(jnp.float32)
            last = jnp.concatenate([last, jnp.zeros((1, 128), jnp.float32)], axis=0)
            total = jnp.sum(block * top, axis=0) + last * tail
            return jnp.sum(total, axis=0, keepdims=True)

        def body(step, carry):
            base = pl.multiple_of(step * 8, 8)
            sums = [row_sum(base + i) for i in range(8)]
            target[pl.ds(base, 8), :] = jnp.concatenate(sums, axis=0)
            return carry

        lax.fori_loop(0, 16, body, 0)
        sums = [row_sum(128 + i) for i in range(7)]
        target[128:135, :] = jnp.concatenate(sums, axis=0)


def on_device(
    inverse,
    start,
    source,
    mass,
    inner_elem,
    inner_face,
    inner_orient,
    inner_jac,
    cross_elem,
    cross_face,
    cross_orient,
    cross_count,
    cross_jac,
):
    count_times = lax.axis_size("tm")
    count_mesh = lax.axis_size("mesh")
    rows, elems = mass.shape
    fin = inner_orient.shape[0]
    slots = cross_elem.shape[1]
    lanes = -(-slots // 128) * 128
    vmem = pl.BlockSpec(memory_space=pltpu.VMEM)
    specs = [vmem] * 13
    specs[0] = pl.BlockSpec(memory_space=pl.ANY)
    specs[11] = pl.BlockSpec(memory_space=pltpu.SMEM)
    result = pl.pallas_call(
        functools.partial(kernel, count_times, count_mesh),
        out_shape=jax.ShapeDtypeStruct((rows, elems), jnp.float32),
        in_specs=specs,
        out_specs=vmem,
        scratch_shapes=[
            pltpu.VMEM((rows, rows, elems), jnp.bfloat16),
            pltpu.VMEM((6 * elems, 2 * fin), jnp.bfloat16),
            pltpu.VMEM((6 * elems, lanes), jnp.bfloat16),
            pltpu.VMEM((8 * NODES, elems), jnp.float32),
            pltpu.VMEM((VARS, 8, 2 * fin + lanes), jnp.float32),
            pltpu.VMEM((8 * NODES, elems), jnp.float32),
            pltpu.VMEM((136, elems), jnp.float32),
            pltpu.VMEM((rows, elems), jnp.float32),
            pltpu.VMEM((SWEEPS, 5, 24, 128), jnp.float32),
            pltpu.VMEM((SWEEPS, 5, 24, 128), jnp.float32),
            pltpu.VMEM((SWEEPS, count_times - 1, rows, elems), jnp.float32),
            pltpu.SemaphoreType.DMA((5,)),
            pltpu.SemaphoreType.DMA((SWEEPS, 5)),
            pltpu.SemaphoreType.DMA((SWEEPS, 5)),
            pltpu.SemaphoreType.DMA((SWEEPS, count_times - 1)),
            pltpu.SemaphoreType.DMA((SWEEPS, count_times - 1)),
        ],
        compiler_params=pltpu.CompilerParams(
            collective_id=0, has_side_effects=True, vmem_limit_bytes=40 * 1024 * 1024
        ),
    )(
        inverse[0],
        start[0],
        source[0],
        mass,
        inner_elem,
        inner_face,
        inner_orient.reshape(1, fin),
        jnp.transpose(inner_jac[0], (1, 0, 2)),
        cross_elem,
        cross_face,
        cross_orient,
        cross_count,
        cross_jac[0],
    )
    return result[None]


def solution(mesh):
    in_specs = (
        P("tm", None, None, "mesh"),
        P("tm", None, "mesh"),
        P("tm", None, "mesh"),
        P(None, "mesh"),
        P(None, "mesh"),
        P(None, "mesh"),
        P("mesh"),
        P("tm", None, None, "mesh"),
        P("mesh", None),
        P("mesh", None),
        P("mesh", None),
        P("mesh", None),
        P("tm", None, "mesh", None),
    )
    out_specs = P("tm", None, "mesh")
    return jax.shard_map(
        on_device, mesh=mesh, in_specs=in_specs, out_specs=out_specs, check_vma=False
    )
```

profile of v0, /device:TPU:0, one launch (start us, length us, event | category | flops | bytes accessed | tf_op | source)
XLA Modules:
  0.0 30.5 jit_solution(4416102234986427806)
XLA Ops:
  0.0 0.9 %copy_bitcast_fusion = (f32[135,128]{1,0:T(8,128)S(1)}, f32[135,128]{1,0:T(8,128)S(1)}) fusion(f32[1,135,128]{2,0,1:T(1,128)} %param.15, f32[1,135,128]{2,0,1:T(1,128)} %param.14), kind=kLoop, calls=%fused_computation | loop fusion | bytes 276480
  0.9 0.0 copy-start
  0.9 2.3 %copy-done = bf16[1,135,135,128]{3,2,1,0:T(8,128)(2,1)S(1)} copy-done((bf16[1,135,135,128]{3,2,1,0:T(8,128)(2,1)S(1)}, bf16[1,135,135,128]{3,2,1,0:T(8,128)(2,1)}, u32[]{:S(2)}) %copy-start) | copy-done | bytes 4665624
  3.3 0.0 copy-start.1
  3.3 0.9 %copy-done.1 = f32[135,128]{1,0:T(8,128)S(1)} copy-done((f32[135,128]{1,0:T(8,128)S(1)}, f32[135,128]{1,0:T(8,128)}, u32[]{:S(2)}) %copy-start.1) | copy-done | bytes 69144
  4.1 0.0 copy-start.2
  4.1 0.8 %copy-done.2 = f32[1,2,25,256]{3,1,2,0:T(2,128)S(1)} copy-done((f32[1,2,25,256]{3,1,2,0:T(2,128)S(1)}, f32[1,2,25,256]{3,1,2,0:T(2,128)}, u32[]{:S(2)}) %copy-start.2) | copy-done | bytes 51224
  5.0 0.0 copy-start.3
  5.0 0.7 %copy-done.3 = f32[1,25,1,160]{3,2,1,0:T(1,128)S(1)} copy-done((f32[1,25,1,160]{3,2,1,0:T(1,128)S(1)}, f32[1,25,1,160]{3,2,1,0:T(1,128)}, u32[]{:S(2)}) %copy-start.3) | copy-done | bytes 16024
  5.7 0.0 copy-start.4
  5.7 0.7 %copy-done.4 = s32[2,256]{1,0:T(2,128)S(1)} copy-done((s32[2,256]{1,0:T(2,128)S(1)}, s32[2,256]{1,0:T(2,128)}, u32[]{:S(2)}) %copy-start.4) | copy-done | bytes 2072
  6.4 0.0 copy-start.5
  6.4 0.7 %copy-done.5 = s32[2,256]{1,0:T(2,128)S(1)} copy-done((s32[2,256]{1,0:T(2,128)S(1)}, s32[2,256]{1,0:T(2,128)}, u32[]{:S(2)}) %copy-start.5) | copy-done | bytes 2072
  7.1 0.0 copy-start.6
  7.1 0.7 %copy-done.6 = s32[256]{0:T(256)S(1)} copy-done((s32[256]{0:T(256)S(1)}, s32[256]{0:T(256)}, u32[]{:S(2)}) %copy-start.6) | copy-done | bytes 1048
  7.7 0.0 copy-start.7
  7.7 0.7 %copy-done.7 = s32[1,160]{1,0:T(1,128)S(1)} copy-done((s32[1,160]{1,0:T(1,128)S(1)}, s32[1,160]{1,0:T(1,128)}, u32[]{:S(2)}) %copy-start.7) | copy-done | bytes 664
  8.4 0.0 copy-start.8
  8.4 0.7 %copy-done.8 = s32[1,160]{1,0:T(1,128)S(1)} copy-done((s32[1,160]{1,0:T(1,128)S(1)}, s32[1,160]{1,0:T(1,128)}, u32[]{:S(2)}) %copy-start.8) | copy-done | bytes 664
  9.1 0.0 copy-start.9
  9.1 0.7 %copy-done.9 = s32[1,160]{1,0:T(1,128)S(1)} copy-done((s32[1,160]{1,0:T(1,128)S(1)}, s32[1,160]{1,0:T(1,128)}, u32[]{:S(2)}) %copy-start.9) | copy-done | bytes 664
  9.8 0.0 copy-start.10
  9.8 0.7 %copy-done.10 = s32[1,5]{1,0:T(1,128)S(1)} copy-done((s32[1,5]{1,0:T(1,128)S(1)}, s32[1,5]{1,0:T(1,128)}, u32[]{:S(2)}) %copy-start.10) | copy-done | bytes 44
  10.4 19.3 %shard_map.127 = f32[135,128]{1,0:T(8,128)S(1)} custom-call(bf16[135,135,128]{2,1,0:T(8,128)(2,1)S(1)} %bitcast.11, f32[135,128]{1,0:T(8,128)S(1)} %get-tuple-element.6.start, f32[135,128]{1,0:T(8,128)S(1)} %get-tuple-element.5.source, f32[135,128]{1,0:T(8,128)S(1)} %copy-done.1, s32[2,256]{1,0:T(2,128)S(1)} %copy-done.4, s32[2,256]{1,0:T(2,128)S(1)} %copy-done.5, ...), custom_call_target="tpu_custom_call" | custom-call | tf_op jit(solution)/shard_map/pallas_call | solution.py:377
  29.8 0.7 %copy.14 = f32[1,135,128]{2,0,1:T(1,128)} copy(f32[1,135,128]{2,1,0:T(8,128)S(1)} %bitcast.12) | data formatting | bytes 138240 | tf_op jit(solution)/shard_map/broadcast_in_dim | solution.py:418
Async XLA Ops:
  0.9 2.3 %copy-start = (bf16[1,135,135,128]{3,2,1,0:T(8,128)(2,1)S(1)}, bf16[1,135,135,128]{3,2,1,0:T(8,128)(2,1)}, u32[]{:S(2)}) copy-start(bf16[1,135,135,128]{3,2,1,0:T(8,128)(2,1)} %param.13) | copy-start | bytes 13996804
  3.3 0.9 %copy-start.1 = (f32[135,128]{1,0:T(8,128)S(1)}, f32[135,128]{1,0:T(8,128)}, u32[]{:S(2)}) copy-start(f32[135,128]{1,0:T(8,128)} %mass.1) | copy-start | bytes 207364
  4.1 0.8 %copy-start.2 = (f32[1,2,25,256]{3,1,2,0:T(2,128)S(1)}, f32[1,2,25,256]{3,1,2,0:T(2,128)}, u32[]{:S(2)}) copy-start(f32[1,2,25,256]{3,1,2,0:T(2,128)} %param.20) | copy-start | bytes 153604
  5.0 0.7 %copy-start.3 = (f32[1,25,1,160]{3,2,1,0:T(1,128)S(1)}, f32[1,25,1,160]{3,2,1,0:T(1,128)}, u32[]{:S(2)}) copy-start(f32[1,25,1,160]{3,2,1,0:T(1,128)} %param.25) | copy-start | bytes 48004
  5.7 0.7 %copy-start.4 = (s32[2,256]{1,0:T(2,128)S(1)}, s32[2,256]{1,0:T(2,128)}, u32[]{:S(2)}) copy-start(s32[2,256]{1,0:T(2,128)} %inner_elem.1) | copy-start | bytes 6148
  6.4 0.7 %copy-start.5 = (s32[2,256]{1,0:T(2,128)S(1)}, s32[2,256]{1,0:T(2,128)}, u32[]{:S(2)}) copy-start(s32[2,256]{1,0:T(2,128)} %inner_face.1) | copy-start | bytes 6148
  7.1 0.7 %copy-start.6 = (s32[256]{0:T(256)S(1)}, s32[256]{0:T(256)}, u32[]{:S(2)}) copy-start(s32[256]{0:T(256)} %param.19) | copy-start | bytes 3076
  7.7 0.7 %copy-start.7 = (s32[1,160]{1,0:T(1,128)S(1)}, s32[1,160]{1,0:T(1,128)}, u32[]{:S(2)}) copy-start(s32[1,160]{1,0:T(1,128)} %cross_elem.1) | copy-start | bytes 1924
  8.4 0.7 %copy-start.8 = (s32[1,160]{1,0:T(1,128)S(1)}, s32[1,160]{1,0:T(1,128)}, u32[]{:S(2)}) copy-start(s32[1,160]{1,0:T(1,128)} %cross_face.1) | copy-start | bytes 1924
  9.1 0.7 %copy-start.9 = (s32[1,160]{1,0:T(1,128)S(1)}, s32[1,160]{1,0:T(1,128)}, u32[]{:S(2)}) copy-start(s32[1,160]{1,0:T(1,128)} %cross_orient.1) | copy-start | bytes 1924
  9.8 0.7 %copy-start.10 = (s32[1,5]{1,0:T(1,128)S(1)}, s32[1,5]{1,0:T(1,128)}, u32[]{:S(2)}) copy-start(s32[1,5]{1,0:T(1,128)} %cross_count.1) | copy-start | bytes 64
where the time goes:
time: 31 us; the launch traced here: 30.5 us
  Pallas kernels  19.3 us (62%)
  local copies, waits for them, and re-layouts  11.1 us (36%)
    pallas_call x1, Pallas kernels, on_device(): pl.pallas_call(functools.partial(kernel, count_times, count_mesh), out_sh...  19.3 us
    unnamed x23, local copies, waits for them, and re-layouts  10.4 us
    broadcast_in_dim x1, local copies, waits for them, and re-layouts, on_device(): return result[None]  0.7 us

commit v1 on v0

--- a/solution.py
+++ b/solution.py
@@ -93,7 +93,19 @@
     count_times,
     count_mesh,
     inverse,
-    start,
+    start_h,
+    source_h,
+    mass_h,
+    inner_elem_h,
+    inner_face_h,
+    inner_orient_h,
+    inner_jac_h,
+    cross_elem_h,
+    cross_face_h,
+    cross_orient_h,
+    cross_count_h,
+    cross_jac_h,
+    out,
     source,
     mass,
     inner_elem,
@@ -105,7 +117,6 @@
     cross_orient,
     cross_count,
     cross_jac,
-    out,
     inv_v,
     hot_inner,
     hot_cross,
@@ -117,13 +128,14 @@
     send_buf,
     recv_buf,
     peer_buf,
+    load_sem,
     inv_sem,
     send_sem,
     recv_sem,
     peer_send_sem,
     peer_recv_sem,
 ):
-    elems = start.shape[1]
+    elems = mass.shape[1]
     fin = inner_orient.shape[1]
     slots = cross_orient.shape[1]
     cap = slots // 5
@@ -142,6 +154,26 @@
         )
         for c in range(5)
     ]
+    pairs = {
+        "cross_face": (cross_face_h, cross_face),
+        "cross_elem": (cross_elem_h, cross_elem),
+        "start": (start_h.at[:, 0], current),
+        "inner_face": (inner_face_h, inner_face),
+        "inner_elem": (inner_elem_h, inner_elem),
+        "inner_orient": (inner_orient_h, inner_orient),
+        "inner_jac": (inner_jac_h, inner_jac),
+        "cross_orient": (cross_orient_h, cross_orient),
+        "cross_count": (cross_count_h, cross_count),
+        "cross_jac": (cross_jac_h, cross_jac),
+        "source": (source_h.at[:, 0], source),
+        "mass": (mass_h, mass),
+    }
+    arrays = {
+        name: pltpu.make_async_copy(src, dst, load_sem.at[index])
+        for index, (name, (src, dst)) in enumerate(pairs.items())
+    }
+    for load in arrays.values():
+        load.start()
     for load in loads:
         load.start()
 
@@ -151,52 +183,61 @@
     for peer in peers:
         pl.semaphore_signal(barrier, inc=1, device_id={"tm": peer}, device_id_type=MESH)
 
+    state[...] = jnp.zeros_like(state)
+    resid[...] = jnp.zeros_like(resid)
+    jac[...] = jnp.zeros_like(jac)
+    zero_tile = jnp.zeros((8, 128), jnp.float32)
+    group = lax.broadcasted_iota(jnp.int32, (8, 128), 1) // cap
+    row = lax.broadcasted_iota(jnp.int32, (8, 128), 0)
+
+    arrays["cross_face"].wait()
+    arrays["cross_elem"].wait()
     cross_key = cross_face[...] * elems + cross_elem[...]
     cross_key = jnp.concatenate(
         [cross_key, jnp.full((1, lanes - slots), -1, jnp.int32)], axis=1
     )
-    inner_key = inner_face[...] * elems + inner_elem[...]
-    inner_key = jnp.concatenate([inner_key[0:1], inner_key[1:2]], axis=1)
     for face in range(6):
         rows = lax.broadcasted_iota(jnp.int32, (elems, lanes), 0) + face * elems
         hot_cross[pl.ds(face * elems, elems), :] = jnp.where(
             rows == cross_key, 1.0, 0.0
         ).astype(jnp.bfloat16)
-        rows = lax.broadcasted_iota(jnp.int32, (elems, 2 * fin), 0) + face * elems
-        hot_inner[pl.ds(face * elems, elems), :] = jnp.where(
-            rows == inner_key, 1.0, 0.0
-        ).astype(jnp.bfloat16)
-
-    jac[...] = jnp.zeros_like(jac)
-    for u in range(VARS):
+    arrays["start"].wait()
+
+    def prepare_inner():
+        for name in ("inner_face", "inner_elem", "inner_orient", "inner_jac"):
+            arrays[name].wait()
+        for name in ("cross_orient", "cross_count", "cross_jac"):
+            arrays[name].wait()
+        inner_key = inner_face[...] * elems + inner_elem[...]
+        inner_key = jnp.concatenate([inner_key[0:1], inner_key[1:2]], axis=1)
+        for face in range(6):
+            rows = lax.broadcasted_iota(jnp.int32, (elems, 2 * fin), 0) + face * elems
+            hot_inner[pl.ds(face * elems, elems), :] = jnp.where(
+                rows == inner_key, 1.0, 0.0
+            ).astype(jnp.bfloat16)
+        for u in range(VARS):
+            for v in range(VARS):
+                jac[u, v : v + 1, 0:fin] = inner_jac[5 * u + v, 0:1, :]
+                jac[u, v : v + 1, fin : 2 * fin] = inner_jac[5 * u + v, 1:2, :]
+                jac[u, v : v + 1, 2 * fin : 2 * fin + slots] = cross_jac[5 * u + v, :, :]
+        orient = inner_orient[...]
+        inner_orients = jnp.concatenate([orient, orient_back(orient)], axis=1)
+        cross_orients = jnp.concatenate(
+            [cross_orient[...], jnp.zeros((1, lanes - slots), jnp.int32)], axis=1
+        )
+        lane = lax.broadcasted_iota(jnp.int32, (1, lanes), 1)
+        live = jnp.zeros((1, lanes), jnp.int32)
+        for k in range(5):
+            live = jnp.where((lane >= k * cap) & (lane < k * cap + cross_count[0, k]), 1, live)
+        live = jnp.broadcast_to(live == 1, (8, lanes))
+        return inner_orients, cross_orients, live
+
+    for sweep in range(SWEEPS):
         for v in range(VARS):
-            jac[u, v : v + 1, 0:fin] = inner_jac[5 * u + v, 0:1, :]
-            jac[u, v : v + 1, fin : 2 * fin] = inner_jac[5 * u + v, 1:2, :]
-            jac[u, v : v + 1, 2 * fin : 2 * fin + slots] = cross_jac[5 * u + v, :, :]
-
-    orient = inner_orient[...]
-    inner_orients = jnp.concatenate([orient, orient_back(orient)], axis=1)
-    cross_orients = jnp.concatenate(
-        [cross_orient[...], jnp.zeros((1, lanes - slots), jnp.int32)], axis=1
-    )
-    lane = lax.broadcasted_iota(jnp.int32, (1, lanes), 1)
-    live = jnp.zeros((1, lanes), jnp.int32)
-    for k in range(5):
-        live = jnp.where((lane >= k * cap) & (lane < k * cap + cross_count[0, k]), 1, live)
-    live = jnp.broadcast_to(live == 1, (8, lanes))
-    group = lax.broadcasted_iota(jnp.int32, (8, 128), 1) // cap
-
-    state[...] = jnp.zeros_like(state)
-    resid[...] = jnp.zeros_like(resid)
-    zero_tile = jnp.zeros((8, 128), jnp.float32)
-
-    for sweep in range(SWEEPS):
-        now = start if sweep == 0 else current
-        for v in range(VARS):
-            state[pl.ds(v, NODES, stride=8), :] = now[v * NODES : (v + 1) * NODES, :]
+            state[pl.ds(v, NODES, stride=8), :] = current[v * NODES : (v + 1) * NODES, :]
         peer_copies = [
             pltpu.make_async_remote_copy(
-                src_ref=now,
+                src_ref=current,
                 dst_ref=peer_buf.at[sweep, d],
                 send_sem=peer_send_sem.at[sweep, d],
                 recv_sem=peer_recv_sem.at[sweep, d],
@@ -224,15 +265,18 @@
         cross_trace = cross_trace[0:72] + cross_trace[72:144]
         for k in range(5):
             column = (k // 4) * 128
-            for h in range(3):
+            last = cross_trace[64:72, column : column + 128]
+            last = pltpu.roll(last, -k % 4 * cap, 1) if k % 4 else last
+            for h in range(2):
                 packed = zero_tile
                 for g in range(4):
                     n = 4 * h + g
-                    if n < 9:
-                        piece = cross_trace[8 * n : 8 * n + 8, column : column + 128]
-                        shift = (g - k % 4) * cap % 128
-                        piece = pltpu.roll(piece, shift, 1) if shift else piece
-                        packed = jnp.where(group == g, piece, packed)
+                    piece = cross_trace[8 * n : 8 * n + 8, column : column + 128]
+                    shift = (g - k % 4) * cap % 128
+                    piece = pltpu.roll(piece, shift, 1) if shift else piece
+                    packed = jnp.where(group == g, piece, packed)
+                extra = pltpu.roll(last, 5 if h == 0 else 2, 0)
+                packed = jnp.where(row >= VARS, extra, packed)
                 send_buf[sweep, k, 8 * h : 8 * h + 8, :] = packed
         if sweep == 0:
             pl.semaphore_wait(barrier, 5 + count_times - 1)
@@ -252,6 +296,7 @@
         if sweep == 0:
             for copy in peer_copies:
                 copy.start()
+            inner_orients, cross_orients, live = prepare_inner()
 
         trace = jnp.dot(faces, hot_inner[...], preferred_element_type=jnp.float32)
         trace = trace[0:72] + trace[72:144]
@@ -276,10 +321,13 @@
             copy.wait_recv()
         arrived = []
         for n in range(9):
-            h, g = n // 4, n % 4
+            h, g = n // 4 % 2, n % 4
             columns = [zero_tile] * (lanes // 128)
             for k in range(5):
                 piece = recv_buf[sweep, k, 8 * h : 8 * h + 8, :]
+                if n == 8:
+                    other = recv_buf[sweep, k, 8:16, :]
+                    piece = jnp.where(row < 3, pltpu.roll(piece, 3, 0), pltpu.roll(other, 6, 0))
                 shift = (k % 4 - g) * cap % 128
                 piece = pltpu.roll(piece, shift, 1) if shift else piece
                 columns[k // 4] = jnp.where(group == k % 4, piece, columns[k // 4])
@@ -306,6 +354,9 @@
         for node in range(NODES):
             couple[8 * node : 8 * node + 8, :] = totals[node]
 
+        if sweep == 0:
+            arrays["source"].wait()
+            arrays["mass"].wait()
         for copy in peer_copies:
             copy.wait_recv()
         for v in range(VARS):
@@ -371,15 +422,24 @@
     slots = cross_elem.shape[1]
     lanes = -(-slots // 128) * 128
     vmem = pl.BlockSpec(memory_space=pltpu.VMEM)
-    specs = [vmem] * 13
-    specs[0] = pl.BlockSpec(memory_space=pl.ANY)
-    specs[11] = pl.BlockSpec(memory_space=pltpu.SMEM)
+    specs = [pl.BlockSpec(memory_space=pl.ANY)] * 13
     result = pl.pallas_call(
         functools.partial(kernel, count_times, count_mesh),
         out_shape=jax.ShapeDtypeStruct((rows, elems), jnp.float32),
         in_specs=specs,
         out_specs=vmem,
         scratch_shapes=[
+            pltpu.VMEM((rows, elems), jnp.float32),
+            pltpu.VMEM((rows, elems), jnp.float32),
+            pltpu.VMEM((2, fin), jnp.int32),
+            pltpu.VMEM((2, fin), jnp.int32),
+            pltpu.VMEM((1, fin), jnp.int32),
+            pltpu.VMEM((25, 2, fin), jnp.float32),
+            pltpu.VMEM((1, slots), jnp.int32),
+            pltpu.VMEM((1, slots), jnp.int32),
+            pltpu.VMEM((1, slots), jnp.int32),
+            pltpu.SMEM((1, 5), jnp.int32),
+            pltpu.VMEM((25, 1, slots), jnp.float32),
             pltpu.VMEM((rows, rows, elems), jnp.bfloat16),
             pltpu.VMEM((6 * elems, 2 * fin), jnp.bfloat16),
             pltpu.VMEM((6 * elems, lanes), jnp.bfloat16),
@@ -388,9 +448,10 @@
             pltpu.VMEM((8 * NODES, elems), jnp.float32),
             pltpu.VMEM((136, elems), jnp.float32),
             pltpu.VMEM((rows, elems), jnp.float32),
-            pltpu.VMEM((SWEEPS, 5, 24, 128), jnp.float32),
-            pltpu.VMEM((SWEEPS, 5, 24, 128), jnp.float32),
+            pltpu.VMEM((SWEEPS, 5, 16, 128), jnp.float32),
+            pltpu.VMEM((SWEEPS, 5, 16, 128), jnp.float32),
             pltpu.VMEM((SWEEPS, count_times - 1, rows, elems), jnp.float32),
+            pltpu.SemaphoreType.DMA((12,)),
             pltpu.SemaphoreType.DMA((5,)),
             pltpu.SemaphoreType.DMA((SWEEPS, 5)),
             pltpu.SemaphoreType.DMA((SWEEPS, 5)),
@@ -398,12 +459,12 @@
             pltpu.SemaphoreType.DMA((SWEEPS, count_times - 1)),
         ],
         compiler_params=pltpu.CompilerParams(
-            collective_id=0, has_side_effects=True, vmem_limit_bytes=40 * 1024 * 1024
+            collective_id=0, has_side_effects=True, vmem_limit_bytes=60 * 1024 * 1024
         ),
     )(
         inverse[0],
-        start[0],
-        source[0],
+        jnp.transpose(start, (1, 0, 2)),
+        jnp.transpose(source, (1, 0, 2)),
         mass,
         inner_elem,
         inner_face,

time: 31 us -> 19.7 us (0.64); the launches traced: 30.5 us -> 19.5 us
  local copies, waits for them, and re-layouts: 11.1 us -> 1.59 us
  Pallas kernels: 19.3 us -> 17.9 us
    unnamed x23 -> x0, local copies, waits for them, and re-layouts: 10.4 us -> none
    pallas_call x1, Pallas kernels: 19.3 us -> 17.9 us  [on_device(): pl.pallas_call(functools.partial(kernel, count_times, count_mesh), out_sh...]
    broadcast_in_dim x1, local copies, waits for them, and re-layouts: 0.7 us -> 1.59 us  [on_device(): return result[None]]
where the time goes in v1:
time: 19.7 us; the launch traced here: 19.5 us
  Pallas kernels  17.9 us (91%)
  local copies, waits for them, and re-layouts  1.59 us (8%)
    pallas_call x1, Pallas kernels, on_device(): pl.pallas_call(functools.partial(kernel, count_times, count_mesh), out_sh...  17.9 us
    broadcast_in_dim x1, local copies, waits for them, and re-layouts, on_device(): return result[None]  1.59 us

profile of v1, /device:TPU:0, one launch (start us, length us, event | category | flops | bytes accessed | tf_op | source)
XLA Modules:
  0.0 19.5 jit_solution(130857719455811470)
XLA Ops:
  0.0 17.9 %shard_map.127 = f32[135,128]{1,0:T(8,128)} custom-call(bf16[135,135,128]{2,1,0:T(8,128)(2,1)} %bitcast.9, f32[135,1,128]{2,1,0:T(1,128)} %bitcast.11, f32[135,1,128]{2,1,0:T(1,128)} %bitcast.12, f32[135,128]{1,0:T(8,128)} %mass_h.1, s32[2,256]{1,0:T(2,128)} %inner_elem_h.1, s32[2,256]{1,0:T(2,128)} %inner_face_h.1, s32[1,256]{1,0:T(1,128)} %bitcast.15, ...), custom_call_target="tpu_custom_call" | custom-call | tf_op jit(solution)/shard_map/pallas_call | solution.py:426
  17.9 1.6 %copy.14 = f32[1,135,128]{2,0,1:T(1,128)} copy(f32[1,135,128]{2,1,0:T(8,128)} %bitcast.10) | data formatting | bytes 138240 | tf_op jit(solution)/shard_map/broadcast_in_dim | solution.py:479

commit v2 on v1

--- a/solution.py
+++ b/solution.py
@@ -125,6 +125,9 @@
     couple,
     resid,
     current,
+    inner_orients,
+    cross_orients,
+    alive,
     send_buf,
     recv_buf,
     peer_buf,
@@ -135,12 +138,12 @@
     peer_send_sem,
     peer_recv_sem,
 ):
-    elems = mass.shape[1]
+    total_rows, elems = mass.shape
     fin = inner_orient.shape[1]
     slots = cross_orient.shape[1]
     cap = slots // 5
     lanes = hot_cross.shape[1]
-    chunk = inv_v.shape[0] // 5
+    chunk = total_rows // 5
     me = lax.axis_index("mesh")
     mine = lax.axis_index("tm")
     offsets = [1, count_mesh - 1, count_mesh // 2 - 1, count_mesh // 2, count_mesh // 2 + 1]
@@ -157,7 +160,7 @@
     pairs = {
         "cross_face": (cross_face_h, cross_face),
         "cross_elem": (cross_elem_h, cross_elem),
-        "start": (start_h.at[:, 0], current),
+        "start": (start_h.at[:, 0], current.at[pl.ds(0, total_rows)]),
         "inner_face": (inner_face_h, inner_face),
         "inner_elem": (inner_elem_h, inner_elem),
         "inner_orient": (inner_orient_h, inner_orient),
@@ -221,23 +224,20 @@
                 jac[u, v : v + 1, fin : 2 * fin] = inner_jac[5 * u + v, 1:2, :]
                 jac[u, v : v + 1, 2 * fin : 2 * fin + slots] = cross_jac[5 * u + v, :, :]
         orient = inner_orient[...]
-        inner_orients = jnp.concatenate([orient, orient_back(orient)], axis=1)
-        cross_orients = jnp.concatenate(
+        inner_orients[...] = jnp.concatenate([orient, orient_back(orient)], axis=1)
+        cross_orients[...] = jnp.concatenate(
             [cross_orient[...], jnp.zeros((1, lanes - slots), jnp.int32)], axis=1
         )
         lane = lax.broadcasted_iota(jnp.int32, (1, lanes), 1)
         live = jnp.zeros((1, lanes), jnp.int32)
         for k in range(5):
             live = jnp.where((lane >= k * cap) & (lane < k * cap + cross_count[0, k]), 1, live)
-        live = jnp.broadcast_to(live == 1, (8, lanes))
-        return inner_orients, cross_orients, live
-
-    for sweep in range(SWEEPS):
-        for v in range(VARS):
-            state[pl.ds(v, NODES, stride=8), :] = current[v * NODES : (v + 1) * NODES, :]
-        peer_copies = [
+        alive[...] = live
+
+    def send_peers(sweep):
+        return [
             pltpu.make_async_remote_copy(
-                src_ref=current,
+                src_ref=current.at[pl.ds(0, total_rows)],
                 dst_ref=peer_buf.at[sweep, d],
                 send_sem=peer_send_sem.at[sweep, d],
                 recv_sem=peer_recv_sem.at[sweep, d],
@@ -246,9 +246,13 @@
             )
             for d in range(count_times - 1)
         ]
-        if sweep > 0:
-            for copy in peer_copies:
-                copy.start()
+
+    def one_sweep(sweep, carry):
+        first = sweep == 0
+
+        for v in range(VARS):
+            state[pl.ds(v, NODES, stride=8), :] = current[v * NODES : (v + 1) * NODES, :]
+        peer_copies = send_peers(sweep)
         tiles = [
             state[8 * node : 8 * node + 8, :] * NODE_WEIGHT[node] for node in range(NODES)
         ]
@@ -278,8 +282,11 @@
                 extra = pltpu.roll(last, 5 if h == 0 else 2, 0)
                 packed = jnp.where(row >= VARS, extra, packed)
                 send_buf[sweep, k, 8 * h : 8 * h + 8, :] = packed
-        if sweep == 0:
+
+        @pl.when(first)
+        def _():
             pl.semaphore_wait(barrier, 5 + count_times - 1)
+
         copies = [
             pltpu.make_async_remote_copy(
                 src_ref=send_buf.at[sweep, k],
@@ -293,10 +300,12 @@
         ]
         for k in (3, 2, 4, 0, 1):
             copies[k].start()
-        if sweep == 0:
+
+        @pl.when(first)
+        def _():
             for copy in peer_copies:
                 copy.start()
-            inner_orients, cross_orients, live = prepare_inner()
+            prepare_inner()
 
         trace = jnp.dot(faces, hot_inner[...], preferred_element_type=jnp.float32)
         trace = trace[0:72] + trace[72:144]
@@ -306,7 +315,7 @@
             )
             for n in range(9)
         ]
-        trace = apply_orient(trace, inner_orients)
+        trace = apply_orient(trace, inner_orients[...])
         received = apply_jacobian([jac[u, :, 0 : 2 * fin] for u in range(VARS)], trace)
         received = split_rows(jnp.concatenate(received, axis=0))
         placed = lax.dot_general(
@@ -332,8 +341,9 @@
                 piece = pltpu.roll(piece, shift, 1) if shift else piece
                 columns[k // 4] = jnp.where(group == k % 4, piece, columns[k // 4])
             arrived.append(jnp.concatenate(columns, axis=1))
-        arrived = apply_orient(arrived, cross_orients)
+        arrived = apply_orient(arrived, cross_orients[...])
         received = apply_jacobian([jac[u, :, 2 * fin :] for u in range(VARS)], arrived)
+        live = jnp.broadcast_to(alive[...] == 1, (8, lanes))
         received = [jnp.where(live, value, 0.0) for value in received]
         received = split_rows(jnp.concatenate(received, axis=0))
         placed = lax.dot_general(
@@ -354,7 +364,9 @@
         for node in range(NODES):
             couple[8 * node : 8 * node + 8, :] = totals[node]
 
-        if sweep == 0:
+
+        @pl.when(first)
+        def _():
             arrays["source"].wait()
             arrays["mass"].wait()
         for copy in peer_copies:
@@ -375,10 +387,12 @@
             copy.wait_send()
         for copy in copies:
             copy.wait_send()
-        if sweep == 0:
+
+        @pl.when(first)
+        def _():
             for load in loads:
                 load.wait()
-        target = out if sweep == SWEEPS - 1 else current
+
         top = resid[0:128, :].reshape(16, 8, 128)
         tail = resid[128:136, :]
 
@@ -392,12 +406,20 @@
         def body(step, carry):
             base = pl.multiple_of(step * 8, 8)
             sums = [row_sum(base + i) for i in range(8)]
-            target[pl.ds(base, 8), :] = jnp.concatenate(sums, axis=0)
+            current[pl.ds(base, 8), :] = jnp.concatenate(sums, axis=0)
             return carry
 
-        lax.fori_loop(0, 16, body, 0)
-        sums = [row_sum(128 + i) for i in range(7)]
-        target[128:135, :] = jnp.concatenate(sums, axis=0)
+        lax.fori_loop(0, (total_rows + 1) // 8, body, 0)
+
+        @pl.when(sweep < SWEEPS - 1)
+        def _():
+            for copy in send_peers(sweep + 1):
+                copy.start()
+
+        return carry
+
+    lax.fori_loop(0, SWEEPS, one_sweep, 0)
+    out[...] = current[0:total_rows, :]
 
 
 def on_device(
@@ -422,7 +444,7 @@
     slots = cross_elem.shape[1]
     lanes = -(-slots // 128) * 128
     vmem = pl.BlockSpec(memory_space=pltpu.VMEM)
-    specs = [pl.BlockSpec(memory_space=pl.ANY)] * 13
+    specs = [pl.BlockSpec(memory_space=pltpu.HBM)] * 13
     result = pl.pallas_call(
         functools.partial(kernel, count_times, count_mesh),
         out_shape=jax.ShapeDtypeStruct((rows, elems), jnp.float32),
@@ -440,14 +462,17 @@
             pltpu.VMEM((1, slots), jnp.int32),
             pltpu.SMEM((1, 5), jnp.int32),
             pltpu.VMEM((25, 1, slots), jnp.float32),
-            pltpu.VMEM((rows, rows, elems), jnp.bfloat16),
+            pltpu.VMEM((rows + 1, rows, elems), jnp.bfloat16),
             pltpu.VMEM((6 * elems, 2 * fin), jnp.bfloat16),
             pltpu.VMEM((6 * elems, lanes), jnp.bfloat16),
             pltpu.VMEM((8 * NODES, elems), jnp.float32),
             pltpu.VMEM((VARS, 8, 2 * fin + lanes), jnp.float32),
             pltpu.VMEM((8 * NODES, elems), jnp.float32),
-            pltpu.VMEM((136, elems), jnp.float32),
-            pltpu.VMEM((rows, elems), jnp.float32),
+            pltpu.VMEM((rows + 1, elems), jnp.float32),
+            pltpu.VMEM((rows + 1, elems), jnp.float32),
+            pltpu.VMEM((1, 2 * fin), jnp.int32),
+            pltpu.VMEM((1, lanes), jnp.int32),
+            pltpu.VMEM((1, lanes), jnp.int32),
             pltpu.VMEM((SWEEPS, 5, 16, 128), jnp.float32),
             pltpu.VMEM((SWEEPS, 5, 16, 128), jnp.float32),
             pltpu.VMEM((SWEEPS, count_times - 1, rows, elems), jnp.float32),
@@ -459,22 +484,27 @@
             pltpu.SemaphoreType.DMA((SWEEPS, count_times - 1)),
         ],
         compiler_params=pltpu.CompilerParams(
-            collective_id=0, has_side_effects=True, vmem_limit_bytes=60 * 1024 * 1024
+            collective_id=0, has_side_effects=True, vmem_limit_bytes=32 * 1024 * 1024
         ),
     )(
-        inverse[0],
-        jnp.transpose(start, (1, 0, 2)),
-        jnp.transpose(source, (1, 0, 2)),
-        mass,
-        inner_elem,
-        inner_face,
-        inner_orient.reshape(1, fin),
-        jnp.transpose(inner_jac[0], (1, 0, 2)),
-        cross_elem,
-        cross_face,
-        cross_orient,
-        cross_count,
-        cross_jac[0],
+        *[
+            pltpu.with_memory_space_constraint(operand, pltpu.HBM)
+            for operand in (
+                inverse[0],
+                jnp.transpose(start, (1, 0, 2)),
+                jnp.transpose(source, (1, 0, 2)),
+                mass,
+                inner_elem,
+                inner_face,
+                inner_orient.reshape(1, fin),
+                jnp.transpose(inner_jac[0], (1, 0, 2)),
+                cross_elem,
+                cross_face,
+                cross_orient,
+                cross_count,
+                cross_jac[0],
+            )
+        ]
     )
     return result[None]
 

time: 19.7 us -> 18.2 us (0.924)
  local copies, waits for them, and re-layouts: 1.59 us -> 0.7 us
  Pallas kernels: 17.9 us -> 17.3 us
    broadcast_in_dim x1, local copies, waits for them, and re-layouts: 1.59 us -> 0.7 us  [on_device(): return result[None]]
    pallas_call x1, Pallas kernels: 17.9 us -> 17.3 us  [on_device(): pl.pallas_call(functools.partial(kernel, count_times, count_mesh), out_sh...]
where the time goes in v2:
time: 18.2 us; the launch traced here: 18 us
  Pallas kernels  17.3 us (95%)
  local copies, waits for them, and re-layouts  0.7 us (4%)
    pallas_call x1, Pallas kernels, on_device(): pl.pallas_call(functools.partial(kernel, count_times, count_mesh), out_sh...  17.3 us
    broadcast_in_dim x1, local copies, waits for them, and re-layouts, on_device(): return result[None]  0.7 us

profile of v2, /device:TPU:0, one launch (start us, length us, event | category | flops | bytes accessed | tf_op | source)
XLA Modules:
  0.0 18.0 jit_solution(18383786745943730744)
XLA Ops:
  0.0 17.3 %shard_map.127 = f32[135,128]{1,0:T(8,128)S(1)} custom-call(bf16[135,135,128]{2,1,0:T(8,128)(2,1)} %bitcast.10, f32[135,1,128]{2,1,0:T(1,128)} %bitcast.11, f32[135,1,128]{2,1,0:T(1,128)} %bitcast.12, f32[135,128]{1,0:T(8,128)} %mass_h.1, s32[2,256]{1,0:T(2,128)} %inner_elem_h.1, s32[2,256]{1,0:T(2,128)} %inner_face_h.1, s32[1,256]{1,0:T(1,128)} %bitcast.15, ...), custom_call_target="tpu_custom_call" | custom-call | tf_op jit(solution)/shard_map/pallas_call | solution.py:448
  17.3 0.7 %copy.14 = f32[1,135,128]{2,0,1:T(1,128)} copy(f32[1,135,128]{2,1,0:T(8,128)S(1)} %bitcast.9) | data formatting | bytes 138240 | tf_op jit(solution)/shard_map/broadcast_in_dim | solution.py:509

commit v3 on v2

--- a/solution.py
+++ b/solution.py
@@ -87,6 +87,17 @@
             total = total + jac[u] * value[u : u + 1, :]
         received.append(total)
     return received
+
+
+def node_sums(placed):
+    totals = [None] * NODES
+    for face in range(6):
+        for n in range(9):
+            node = FACE_NODES[face][n]
+            piece = placed[8 * n : 8 * n + 8, face * 128 : (face + 1) * 128]
+            totals[node] = piece if totals[node] is None else totals[node] + piece
+    zero = jnp.zeros((8, 128), jnp.float32)
+    return [zero if total is None else total for total in totals]
 
 
 def kernel(
@@ -128,6 +139,7 @@
     inner_orients,
     cross_orients,
     alive,
+    partial,
     send_buf,
     recv_buf,
     peer_buf,
@@ -175,16 +187,18 @@
         name: pltpu.make_async_copy(src, dst, load_sem.at[index])
         for index, (name, (src, dst)) in enumerate(pairs.items())
     }
-    for load in arrays.values():
-        load.start()
-    for load in loads:
-        load.start()
+    for name in ("cross_face", "cross_elem", "start"):
+        arrays[name].start()
 
     barrier = pltpu.get_barrier_semaphore()
     for partner in partners:
         pl.semaphore_signal(barrier, inc=1, device_id={"mesh": partner}, device_id_type=MESH)
     for peer in peers:
         pl.semaphore_signal(barrier, inc=1, device_id={"tm": peer}, device_id_type=MESH)
+    for name in list(arrays)[3:]:
+        arrays[name].start()
+    for load in loads:
+        load.start()
 
     state[...] = jnp.zeros_like(state)
     resid[...] = jnp.zeros_like(resid)
@@ -324,7 +338,18 @@
             (((1,), (1,)), ((), ())),
             preferred_element_type=jnp.float32,
         )
-        inner_placed = placed[0:72] + placed[72:144]
+        placed = placed[0:72] + placed[72:144]
+        for node, total in enumerate(node_sums(placed)):
+            couple[8 * node : 8 * node + 8, :] = total
+
+        @pl.when(first)
+        def _():
+            arrays["source"].wait()
+            arrays["mass"].wait()
+
+        for v in range(VARS):
+            rows = slice(v * NODES, (v + 1) * NODES)
+            resid[rows, :] = source[rows, :] - couple[pl.ds(v, NODES, stride=8), :]
 
         for copy in copies:
             copy.wait_recv()
@@ -352,23 +377,10 @@
             (((1,), (1,)), ((), ())),
             preferred_element_type=jnp.float32,
         )
-        placed = placed[0:72] + placed[72:144] + inner_placed
-
-        totals = [zero_tile] * NODES
-        for face in range(6):
-            for n in range(9):
-                node = FACE_NODES[face][n]
-                totals[node] = (
-                    totals[node] + placed[8 * n : 8 * n + 8, face * elems : (face + 1) * elems]
-                )
-        for node in range(NODES):
-            couple[8 * node : 8 * node + 8, :] = totals[node]
-
-
-        @pl.when(first)
-        def _():
-            arrays["source"].wait()
-            arrays["mass"].wait()
+        placed = placed[0:72] + placed[72:144]
+        for node, total in enumerate(node_sums(placed)):
+            couple[8 * node : 8 * node + 8, :] = total
+
         for copy in peer_copies:
             copy.wait_recv()
         for v in range(VARS):
@@ -377,7 +389,7 @@
             for d in range(1, count_times - 1):
                 spectral = spectral + coef[d + 1] * peer_buf[sweep, d, rows, :]
             value = (
-                source[rows, :]
+                resid[rows, :]
                 - couple[pl.ds(v, NODES, stride=8), :]
                 - mass[rows, :] * spectral
             )
@@ -400,16 +412,20 @@
             block = inv_v[row, 0:128, :].astype(jnp.float32).reshape(16, 8, 128)
             last = inv_v[row, 128:135, :].astype(jnp.float32)
             last = jnp.concatenate([last, jnp.zeros((1, 128), jnp.float32)], axis=0)
-            total = jnp.sum(block * top, axis=0) + last * tail
-            return jnp.sum(total, axis=0, keepdims=True)
+            return jnp.sum(block * top, axis=0) + last * tail
 
         def body(step, carry):
-            base = pl.multiple_of(step * 8, 8)
-            sums = [row_sum(base + i) for i in range(8)]
-            current[pl.ds(base, 8), :] = jnp.concatenate(sums, axis=0)
+            for i in range(17):
+                index = step * 17 + i
+                partial[pl.ds(pl.multiple_of(index * 8, 8), 8), :] = row_sum(index)
             return carry
 
-        lax.fori_loop(0, (total_rows + 1) // 8, body, 0)
+        padded = total_rows + 1
+        lax.fori_loop(0, padded // 17, body, 0)
+        total = partial[pl.ds(0, padded, stride=8), :]
+        for i in range(1, 8):
+            total = total + partial[pl.ds(i, padded, stride=8), :]
+        current[...] = total
 
         @pl.when(sweep < SWEEPS - 1)
         def _():
@@ -473,6 +489,7 @@
             pltpu.VMEM((1, 2 * fin), jnp.int32),
             pltpu.VMEM((1, lanes), jnp.int32),
             pltpu.VMEM((1, lanes), jnp.int32),
+            pltpu.VMEM((8 * (rows + 1), elems), jnp.float32),
             pltpu.VMEM((SWEEPS, 5, 16, 128), jnp.float32),
             pltpu.VMEM((SWEEPS, 5, 16, 128), jnp.float32),
             pltpu.VMEM((SWEEPS, count_times - 1, rows, elems), jnp.float32),

time: 18.2 us -> 17.8 us (0.978)
  Pallas kernels: 17.3 us -> 17 us
    pallas_call x1, Pallas kernels: 17.3 us -> 17 us  [on_device(): pl.pallas_call(functools.partial(kernel, count_times, count_mesh), out_sh...]
where the time goes in v3:
time: 17.8 us; the launch traced here: 17.7 us
  Pallas kernels  17 us (96%)
  local copies, waits for them, and re-layouts  0.7 us (4%)
    pallas_call x1, Pallas kernels, on_device(): pl.pallas_call(functools.partial(kernel, count_times, count_mesh), out_sh...  17 us
    broadcast_in_dim x1, local copies, waits for them, and re-layouts, on_device(): return result[None]  0.7 us

profile of v3, /device:TPU:0, one launch (start us, length us, event | category | flops | bytes accessed | tf_op | source)
XLA Modules:
  0.0 17.7 jit_solution(4909830022440813898)
XLA Ops:
  0.0 17.0 %shard_map.127 = f32[135,128]{1,0:T(8,128)S(1)} custom-call(bf16[135,135,128]{2,1,0:T(8,128)(2,1)} %bitcast.10, f32[135,1,128]{2,1,0:T(1,128)} %bitcast.11, f32[135,1,128]{2,1,0:T(1,128)} %bitcast.12, f32[135,128]{1,0:T(8,128)} %mass_h.1, s32[2,256]{1,0:T(2,128)} %inner_elem_h.1, s32[2,256]{1,0:T(2,128)} %inner_face_h.1, s32[1,256]{1,0:T(1,128)} %bitcast.15, ...), custom_call_target="tpu_custom_call" | custom-call | tf_op jit(solution)/shard_map/pallas_call | solution.py:464
  17.0 0.7 %copy.14 = f32[1,135,128]{2,0,1:T(1,128)} copy(f32[1,135,128]{2,1,0:T(8,128)S(1)} %bitcast.9) | data formatting | bytes 138240 | tf_op jit(solution)/shard_map/broadcast_in_dim | solution.py:526

commit v4 on v3

--- a/solution.py
+++ b/solution.py
@@ -131,6 +131,8 @@
     inv_v,
     hot_inner,
     hot_cross,
+    put_inner,
+    put_cross,
     state,
     jac,
     couple,
@@ -232,6 +234,16 @@
             hot_inner[pl.ds(face * elems, elems), :] = jnp.where(
                 rows == inner_key, 1.0, 0.0
             ).astype(jnp.bfloat16)
+        column = lax.broadcasted_iota(jnp.int32, (128, elems), 1)
+        for key, table in ((inner_key, put_inner), (cross_key, put_cross)):
+            for block in range(table.shape[0] // 128):
+                place = slice(block * 128, (block + 1) * 128)
+                spread = jnp.broadcast_to(key[:, place].astype(jnp.float32), (128, 128))
+                spread = spread.T.astype(jnp.int32)
+                for face in range(6):
+                    table[place, face * elems : (face + 1) * elems] = jnp.where(
+                        column == spread - face * elems, 1.0, 0.0
+                    ).astype(jnp.bfloat16)
         for u in range(VARS):
             for v in range(VARS):
                 jac[u, v : v + 1, 0:fin] = inner_jac[5 * u + v, 0:1, :]
@@ -296,11 +308,6 @@
                 extra = pltpu.roll(last, 5 if h == 0 else 2, 0)
                 packed = jnp.where(row >= VARS, extra, packed)
                 send_buf[sweep, k, 8 * h : 8 * h + 8, :] = packed
-
-        @pl.when(first)
-        def _():
-            pl.semaphore_wait(barrier, 5 + count_times - 1)
-
         copies = [
             pltpu.make_async_remote_copy(
                 src_ref=send_buf.at[sweep, k],
@@ -315,11 +322,7 @@
         for k in (3, 2, 4, 0, 1):
             copies[k].start()
 
-        @pl.when(first)
-        def _():
-            for copy in peer_copies:
-                copy.start()
-            prepare_inner()
+        pl.when(first)(prepare_inner)
 
         trace = jnp.dot(faces, hot_inner[...], preferred_element_type=jnp.float32)
         trace = trace[0:72] + trace[72:144]
@@ -332,12 +335,7 @@
         trace = apply_orient(trace, inner_orients[...])
         received = apply_jacobian([jac[u, :, 0 : 2 * fin] for u in range(VARS)], trace)
         received = split_rows(jnp.concatenate(received, axis=0))
-        placed = lax.dot_general(
-            received,
-            hot_inner[...],
-            (((1,), (1,)), ((), ())),
-            preferred_element_type=jnp.float32,
-        )
+        placed = jnp.dot(received, put_inner[...], preferred_element_type=jnp.float32)
         placed = placed[0:72] + placed[72:144]
         for node, total in enumerate(node_sums(placed)):
             couple[8 * node : 8 * node + 8, :] = total
@@ -371,12 +369,7 @@
         live = jnp.broadcast_to(alive[...] == 1, (8, lanes))
         received = [jnp.where(live, value, 0.0) for value in received]
         received = split_rows(jnp.concatenate(received, axis=0))
-        placed = lax.dot_general(
-            received,
-            hot_cross[...],
-            (((1,), (1,)), ((), ())),
-            preferred_element_type=jnp.float32,
-        )
+        placed = jnp.dot(received, put_cross[...], preferred_element_type=jnp.float32)
         placed = placed[0:72] + placed[72:144]
         for node, total in enumerate(node_sums(placed)):
             couple[8 * node : 8 * node + 8, :] = total
@@ -434,6 +427,9 @@
 
         return carry
 
+    pl.semaphore_wait(barrier, 5 + count_times - 1)
+    for copy in send_peers(0):
+        copy.start()
     lax.fori_loop(0, SWEEPS, one_sweep, 0)
     out[...] = current[0:total_rows, :]
 
@@ -481,6 +477,8 @@
             pltpu.VMEM((rows + 1, rows, elems), jnp.bfloat16),
             pltpu.VMEM((6 * elems, 2 * fin), jnp.bfloat16),
             pltpu.VMEM((6 * elems, lanes), jnp.bfloat16),
+            pltpu.VMEM((2 * fin, 6 * elems), jnp.bfloat16),
+            pltpu.VMEM((lanes, 6 * elems), jnp.bfloat16),
             pltpu.VMEM((8 * NODES, elems), jnp.float32),
             pltpu.VMEM((VARS, 8, 2 * fin + lanes), jnp.float32),
             pltpu.VMEM((8 * NODES, elems), jnp.float32),

time: 17.8 us -> 18.2 us (1.022)
  Pallas kernels: 17 us -> 17.3 us
    pallas_call x1, Pallas kernels: 17 us -> 17.3 us  [on_device(): pl.pallas_call(functools.partial(kernel, count_times, count_mesh), out_sh...]
where the time goes in v4:
time: 18.2 us; the launch traced here: 18 us
  Pallas kernels  17.3 us (95%)
  local copies, waits for them, and re-layouts  0.7 us (4%)
    pallas_call x1, Pallas kernels, on_device(): pl.pallas_call(functools.partial(kernel, count_times, count_mesh), out_sh...  17.3 us
    broadcast_in_dim x1, local copies, waits for them, and re-layouts, on_device(): return result[None]  0.7 us

profile of v4, /device:TPU:0, one launch (start us, length us, event | category | flops | bytes accessed | tf_op | source)
XLA Modules:
  0.0 18.0 jit_solution(9972202771585848040)
XLA Ops:
  0.0 17.3 %shard_map.127 = f32[135,128]{1,0:T(8,128)S(1)} custom-call(bf16[135,135,128]{2,1,0:T(8,128)(2,1)} %bitcast.10, f32[135,1,128]{2,1,0:T(1,128)} %bitcast.11, f32[135,1,128]{2,1,0:T(1,128)} %bitcast.12, f32[135,128]{1,0:T(8,128)} %mass_h.1, s32[2,256]{1,0:T(2,128)} %inner_elem_h.1, s32[2,256]{1,0:T(2,128)} %inner_face_h.1, s32[1,256]{1,0:T(1,128)} %bitcast.15, ...), custom_call_target="tpu_custom_call" | custom-call | tf_op jit(solution)/shard_map/pallas_call | solution.py:460
  17.3 0.7 %copy.14 = f32[1,135,128]{2,0,1:T(1,128)} copy(f32[1,135,128]{2,1,0:T(8,128)S(1)} %bitcast.9) | data formatting | bytes 138240 | tf_op jit(solution)/shard_map/broadcast_in_dim | solution.py:524

commit v5 on v3

--- a/solution.py
+++ b/solution.py
@@ -45,11 +45,6 @@
         phase = math.pi * k / count
         table[k] = 0.3 * parity * math.cos(phase) / math.sin(phase) + 1.2 * parity / count
     return [float(np.float32(c)) for c in table]
-
-
-def split_rows(value):
-    high = value.astype(jnp.bfloat16).astype(jnp.float32)
-    return jnp.concatenate([high, value - high], axis=0).astype(jnp.bfloat16)
 
 
 def orient_back(orient):
@@ -277,10 +272,9 @@
             ],
             axis=0,
         )
-        faces = split_rows(faces)
+        faces = faces.astype(jnp.bfloat16)
 
         cross_trace = jnp.dot(faces, hot_cross[...], preferred_element_type=jnp.float32)
-        cross_trace = cross_trace[0:72] + cross_trace[72:144]
         for k in range(5):
             column = (k // 4) * 128
             last = cross_trace[64:72, column : column + 128]
@@ -322,7 +316,6 @@
             prepare_inner()
 
         trace = jnp.dot(faces, hot_inner[...], preferred_element_type=jnp.float32)
-        trace = trace[0:72] + trace[72:144]
         trace = [
             jnp.concatenate(
                 [trace[8 * n : 8 * n + 8, fin:], trace[8 * n : 8 * n + 8, :fin]], axis=1
@@ -331,14 +324,13 @@
         ]
         trace = apply_orient(trace, inner_orients[...])
         received = apply_jacobian([jac[u, :, 0 : 2 * fin] for u in range(VARS)], trace)
-        received = split_rows(jnp.concatenate(received, axis=0))
+        received = jnp.concatenate(received, axis=0).astype(jnp.bfloat16)
         placed = lax.dot_general(
             received,
             hot_inner[...],
             (((1,), (1,)), ((), ())),
             preferred_element_type=jnp.float32,
         )
-        placed = placed[0:72] + placed[72:144]
         for node, total in enumerate(node_sums(placed)):
             couple[8 * node : 8 * node + 8, :] = total
 
@@ -370,14 +362,13 @@
         received = apply_jacobian([jac[u, :, 2 * fin :] for u in range(VARS)], arrived)
         live = jnp.broadcast_to(alive[...] == 1, (8, lanes))
         received = [jnp.where(live, value, 0.0) for value in received]
-        received = split_rows(jnp.concatenate(received, axis=0))
+        received = jnp.concatenate(received, axis=0).astype(jnp.bfloat16)
         placed = lax.dot_general(
             received,
             hot_cross[...],
             (((1,), (1,)), ((), ())),
             preferred_element_type=jnp.float32,
         )
-        placed = placed[0:72] + placed[72:144]
         for node, total in enumerate(node_sums(placed)):
             couple[8 * node : 8 * node + 8, :] = total
 

time: 17.8 us -> 17.8 us (level)
  no operation moved by 1% of the time
where the time goes in v5:
time: 17.8 us; the launch traced here: 17.6 us
  Pallas kernels  16.9 us (95%)
  local copies, waits for them, and re-layouts  0.7 us (4%)
    pallas_call x1, Pallas kernels, on_device(): pl.pallas_call(functools.partial(kernel, count_times, count_mesh), out_sh...  16.9 us
    broadcast_in_dim x1, local copies, waits for them, and re-layouts, on_device(): return result[None]  0.7 us

profile of v5, /device:TPU:0, one launch (start us, length us, event | category | flops | bytes accessed | tf_op | source)
XLA Modules:
  0.0 17.6 jit_solution(14105342413430141187)
XLA Ops:
  0.0 16.9 %shard_map.127 = f32[135,128]{1,0:T(8,128)S(1)} custom-call(bf16[135,135,128]{2,1,0:T(8,128)(2,1)} %bitcast.10, f32[135,1,128]{2,1,0:T(1,128)} %bitcast.11, f32[135,1,128]{2,1,0:T(1,128)} %bitcast.12, f32[135,128]{1,0:T(8,128)} %mass_h.1, s32[2,256]{1,0:T(2,128)} %inner_elem_h.1, s32[2,256]{1,0:T(2,128)} %inner_face_h.1, s32[1,256]{1,0:T(1,128)} %bitcast.15, ...), custom_call_target="tpu_custom_call" | custom-call | tf_op jit(solution)/shard_map/pallas_call | solution.py:455
  16.9 0.7 %copy.14 = f32[1,135,128]{2,0,1:T(1,128)} copy(f32[1,135,128]{2,1,0:T(8,128)S(1)} %bitcast.9) | data formatting | bytes 138240 | tf_op jit(solution)/shard_map/broadcast_in_dim | solution.py:517
